TPU v7x, 256 devices: a whole 4x4x8 slice. The times are simulated.
256 devices in a mesh: freq: 4 (over x), row: 8 (over y, core), col: 8 (over z).
Axes of the slice: x: 4, y: 4, z: 8, core: 2. Of those that a mesh axis runs over, the one named last changes fastest.
Arguments:
- operator: bfloat16 [4, 2, 12000, 12000], P('freq', None, 'row', 'col'), may hold values from -0.0390625 to 0.0390625
- recorded: bfloat16 [4, 2, 12000, 128], P('freq', None, 'row'), may hold values from -61 to 61
Outputs:
- solution: float32 [4, 2, 12000, 128], P('freq', None, 'col')
- residual: float32 [4, 2, 12000, 128], P('freq', None, 'row')
All inputs are finite; a program needn't handle non-finite values.
Results may differ from a plain program's by a relative error of at most 0.0044.
Values sent between devices are 32-bit elements; how exact they have to be, the bound alone decides.
A program may use at most 128 MiB of HBM per device.

v0:
```python
import jax
import jax.numpy as jnp
from jax import lax
from jax.sharding import PartitionSpec as P

ITERS = 2


epsilon = 1e-06


def forward_part(operator, vector):
    blocks = jnp.einsum("krc,lcs->klrs", operator[0], vector[0], preferred_element_type=jnp.float32)
    return jnp.stack([blocks[0, 0] - blocks[1, 1], blocks[0, 1] + blocks[1, 0]])[None]


def adjoint_part(operator, vector):
    blocks = jnp.einsum("krc,lrs->klcs", operator[0], vector[0], preferred_element_type=jnp.float32)
    return jnp.stack([blocks[0, 0] + blocks[1, 1], blocks[0, 1] - blocks[1, 0]])[None]


def forward_reduce(partial_value, left_vec, alpha_now):
    imaged = lax.psum(partial_value, "col")
    update = imaged - alpha_now * left_vec
    squares = lax.psum(jnp.sum(update * update), ("freq", "row"))
    return (imaged, update, jnp.sqrt(squares + epsilon))


def adjoint_reduce(partial_value, right_vec, beta_now):
    summed = lax.psum(partial_value, "row")
    update = summed - beta_now * right_vec
    squares = lax.psum(jnp.sum(update * update), ("freq", "col"))
    return (update, jnp.sqrt(squares + epsilon))


def shards(operator, recorded):
    observed = recorded.astype(jnp.float32)
    col_rows = operator.shape[3]
    sources = recorded.shape[3]
    beta_now = jnp.sqrt(lax.psum(jnp.sum(observed * observed), ("freq", "row")) + epsilon)
    left_vec = observed / beta_now
    right_vec = jnp.zeros((1, 2, col_rows, sources), jnp.float32)
    back, alpha_now = adjoint_reduce(
        adjoint_part(operator, left_vec.astype(jnp.bfloat16)), right_vec, beta_now
    )
    right_vec = back / alpha_now
    search = right_vec
    phi_bar = beta_now
    rho_bar = alpha_now
    solution = jnp.zeros((1, 2, col_rows, sources), jnp.float32)
    fitted = jnp.zeros_like(observed)
    search_image = fitted
    w_ratio = jnp.float32(0.0)
    for turn_index in range(ITERS):
        imaged, update, beta_now = forward_reduce(
            forward_part(operator, right_vec.astype(jnp.bfloat16)), left_vec, alpha_now
        )
        left_vec = update / beta_now
        if turn_index == 0:
            search_image = imaged
        else:
            search_image = imaged - w_ratio * search_image
        rho_now = jnp.sqrt(rho_bar * rho_bar + beta_now * beta_now)
        cosine = rho_bar / rho_now
        sine_val = beta_now / rho_now
        phi_now = cosine * phi_bar
        phi_bar = sine_val * phi_bar
        solution = solution + phi_now / rho_now * search
        fitted = fitted + phi_now / rho_now * search_image
        if turn_index + 1 < ITERS:
            back, alpha_now = adjoint_reduce(
                adjoint_part(operator, left_vec.astype(jnp.bfloat16)), right_vec, beta_now
            )
            right_vec = back / alpha_now
            w_ratio = sine_val * alpha_now / rho_now
            rho_bar = -cosine * alpha_now
            search = right_vec - w_ratio * search
    return (solution, observed - fitted)


def solution(mesh):
    in_specs = (P("freq", None, "row", "col"), P("freq", None, "row", None))
    out_specs = (P("freq", None, "col", None), P("freq", None, "row", None))
    return jax.shard_map(shards, mesh=mesh, in_specs=in_specs, out_specs=out_specs, check_vma=False)
```

profile of v0, /device:TPU:1, one launch (start us, length us, event | category | flops | bytes accessed | tf_op | source)
XLA Modules:
  0.0 721.2 jit_solution(233663717337705087)
XLA Ops:
  7.2 2.1 fusion.20
  9.3 65.9 %psum.63 = f32[]{:T(128)} all-reduce(f32[]{:T(128)} %fusion.20), channel_id=1, replica_groups=mesh['freq'=4,'row'=8,'col'=8] {'freq','row'}, use_global_device_ids=true, to_apply=%region_1.0 | all-reduce | flops 1 | bytes 8 | tf_op jit(solution)/shard_map/psum | solution.py:40
  75.9 23.8 %copy.5 = bf16[2,1500,1500]{1,2,0:T(8,128)(2,1)} copy(bf16[2,1500,1500]{2,0,1:T(2,128)(2,1)} %bitcast.70) | data formatting | bytes 18000000 | tf_op jit(solution)/shard_map/squeeze | solution.py:18
  99.7 6.3 fusion.17
  106.0 0.1 fusion.30
  106.1 0.1 fusion.32
  106.2 1.2 maximum_bitcast_fusion
  107.5 0.0 all-reduce.7.cloned.1.call-start
  107.5 67.9 %all-reduce.5.cloned.1.call-done = f32[1,2,1500,128]{3,2,1,0:T(8,128)} async-done(((f32[1,2,1500,128]{3,2,1,0:T(8,128)}), f32[1,2,1500,128]{3,2,1,0:T(8,128)}) %all-reduce.5.cloned.1.call-update) | async-done | bytes 1536016 | tf_op jit(solution)/shard_map/psum | solution.py:30
  175.4 2.5 multiply_reduce_fusion.3
  177.9 61.5 %psum.65 = f32[]{:T(128)} all-reduce(f32[]{:T(128)} %multiply_reduce_fusion.3), channel_id=1, replica_groups=mesh['freq'=4,'row'=8,'col'=8] {'freq','col'}, use_global_device_ids=true, to_apply=%region_4.0 | all-reduce | flops 1 | bytes 8 | tf_op jit(solution)/shard_map/psum | solution.py:32
  240.1 6.3 fusion.8
  246.5 0.2 fusion.29
  246.6 1.2 maximum_bitcast_fusion.1
  247.9 82.4 %all-reduce.7.cloned.1.call-done = f32[1,2,1500,128]{3,2,1,0:T(8,128)} async-done(((f32[1,2,1500,128]{3,2,1,0:T(8,128)}), f32[1,2,1500,128]{3,2,1,0:T(8,128)}) %all-reduce.7.cloned.1.call-update) | async-done | bytes 1536016 | tf_op jit(solution)/shard_map/psum | solution.py:23
  330.4 2.7 multiply_reduce_fusion.2
  333.1 67.5 %psum.67 = f32[]{:T(128)} all-reduce(f32[]{:T(128)} %multiply_reduce_fusion.2), channel_id=1, replica_groups=mesh['freq'=4,'row'=8,'col'=8] {'freq','row'}, use_global_device_ids=true, to_apply=%region_7.0 | all-reduce | flops 1 | bytes 8 | tf_op jit(solution)/shard_map/psum | solution.py:25
  401.3 8.2 %fusion.14 = f32[2,2,1500,128]{3,2,1,0:T(8,128)S(1)} fusion(bf16[2,1500,1500,1]{2,0,1,3:T(2,128)(2,1)} %bitcast.72, f32[]{:T(128)S(6)} %sqrt.23, f32[1,2,1500,128]{3,2,1,0:T(8,128)S(1)} %copy-done.1, f32[]{:T(128)S(6)} %sqrt.22, f32[]{:T(128)S(6)} %sqrt.21, bf16[1,2,1500,128]{3,1,2,0:T(2,128)(2,1)} %param.3), kind=kOutput, calls=%fused_computation.10 | convolution fusion | flops 2306304000 | bytes 14376012 | tf_op jit(solution)/shard_map/krc,lrs->klcs/dot_general | solution.py:18
  409.5 0.2 fusion.27
  409.6 1.2 maximum_bitcast_fusion.2
  411.0 61.3 %all-reduce.9.cloned.1.call-done = f32[1,2,1500,128]{3,2,1,0:T(8,128)} async-done(((f32[1,2,1500,128]{3,2,1,0:T(8,128)}), f32[1,2,1500,128]{3,2,1,0:T(8,128)}) %all-reduce.9.cloned.1.call-update) | async-done | bytes 1536016 | tf_op jit(solution)/shard_map/psum | solution.py:30
  472.2 2.4 multiply_reduce_fusion.1
  474.6 61.5 %psum.69 = f32[]{:T(128)} all-reduce(f32[]{:T(128)} %multiply_reduce_fusion.1), channel_id=1, replica_groups=mesh['freq'=4,'row'=8,'col'=8] {'freq','col'}, use_global_device_ids=true, to_apply=%region_10.0 | all-reduce | flops 1 | bytes 8 | tf_op jit(solution)/shard_map/psum | solution.py:32
  536.8 6.9 fusion.11
  543.7 0.2 fusion.25
  543.9 1.2 maximum_bitcast_fusion.3
  545.3 82.4 %all-reduce.11.cloned.1.call-done = f32[1,2,1500,128]{3,2,1,0:T(8,128)} async-done(((f32[1,2,1500,128]{3,2,1,0:T(8,128)}), f32[1,2,1500,128]{3,2,1,0:T(8,128)}) %all-reduce.11.cloned.1.call-update) | async-done | bytes 1536016 | tf_op jit(solution)/shard_map/psum | solution.py:23
  627.7 2.6 multiply_reduce_fusion
  630.4 67.6 %psum.71 = f32[]{:T(128)} all-reduce(f32[]{:T(128)} %multiply_reduce_fusion), channel_id=1, replica_groups=mesh['freq'=4,'row'=8,'col'=8] {'freq','row'}, use_global_device_ids=true, to_apply=%region_13.0 | all-reduce | flops 1 | bytes 8 | tf_op jit(solution)/shard_map/psum | solution.py:25
  698.8 3.0 convert_subtract_fusion
  701.8 6.4 copy.14
  708.2 6.4 copy.15
  (13 shorter events, 0.2 us)
Async XLA Ops:
  7.2 168.3 %all-reduce.5.cloned.1.call-start = ((), (), s32[]{:S(2)}) async-start(), calls=%async_computation | async-start | bytes 3080192 | tf_op jit(solution)/shard_map/psum | solution.py:30
  75.9 23.8 %copy-start.2 = (bf16[1,2,1500,128]{3,1,2,0:T(2,128)(2,1)S(1)}, bf16[1,2,1500,128]{3,1,2,0:T(2,128)(2,1)}, u32[]{:S(2)}) copy-start(bf16[1,2,1500,128]{3,1,2,0:T(2,128)(2,1)} %param.3) | copy-start | bytes 2304004
  107.5 222.9 %all-reduce.7.cloned.1.call-start = ((), (), s32[]{:S(2)}) async-start(), calls=%async_computation.1 | async-start | bytes 3080192 | tf_op jit(solution)/shard_map/psum | solution.py:23
  175.4 64.7 %copy-start = (f32[1,2,1500,128]{3,2,1,0:T(8,128)S(1)}, f32[1,2,1500,128]{3,2,1,0:T(8,128)}, u32[]{:S(2)}) copy-start(f32[1,2,1500,128]{3,2,1,0:T(8,128)} %all-reduce.5.cloned.1.call-done) | copy-start | bytes 4608004
  247.9 224.4 %all-reduce.9.cloned.1.call-start = ((), (), s32[]{:S(2)}) async-start(), calls=%async_computation.2 | async-start | bytes 3080192 | tf_op jit(solution)/shard_map/psum | solution.py:30
  330.4 70.9 %copy-start.1 = (f32[1,2,1500,128]{3,2,1,0:T(8,128)S(1)}, f32[1,2,1500,128]{3,2,1,0:T(8,128)}, u32[]{:S(2)}) copy-start(f32[1,2,1500,128]{3,2,1,0:T(8,128)} %all-reduce.7.cloned.1.call-done) | copy-start | bytes 4608004
  410.9 216.8 %all-reduce.11.cloned.1.call-start = ((), (), s32[]{:S(2)}) async-start(), calls=%async_computation.3 | async-start | bytes 3080192 | tf_op jit(solution)/shard_map/psum | solution.py:23
Sparse Core Ops, SparseCore 0:
  107.6 67.7 all-reduce.4
  248.0 82.3 all-reduce.6
  411.0 61.1 all-reduce.8
  545.3 82.3 all-reduce.10
where the time goes:
time: 722 us; the launch traced here: 721 us
  blocking collectives  324 us (45%)
  waiting for transfers between devices  294 us (41%)
  local copies, waits for them, and re-layouts  36.7 us (5%)
  matrix products  27.7 us (4%)
  other arithmetic  20.9 us (3%)
  between operations  17.7 us (2%)
    psum x2, waiting for transfers between devices, forward_reduce(): imaged = lax.psum(partial_value, 'col')  165 us
    psum x2, blocking collectives, forward_reduce(): squares = lax.psum(jnp.sum(update * update), ('freq', 'row'))  135 us
    psum x2, waiting for transfers between devices, adjoint_reduce(): summed = lax.psum(partial_value, 'row')  129 us
    psum x2, blocking collectives, adjoint_reduce(): squares = lax.psum(jnp.sum(update * update), ('freq', 'col'))  123 us
    psum x1, blocking collectives, shards(): lax.psum(jnp.sum(observed * observed), ('freq', 'row')) + epsilon  65.9 us
    squeeze x1, local copies, waits for them, and re-layouts, adjoint_part(): operator[0]  23.8 us
    dot_general x2, matrix products, adjoint_part(): jnp.einsum('krc,lrs->klcs', operator[0], vector[0], preferred_element_typ...  14.5 us
  transfers between devices with their start and end apart: 4, of which 4 were waited for; matrix products, arithmetic and copies ran while one was open for 0% of the time, Pallas kernels for 0%

commit v1 on v0

v1 whole, which is shorter than its diff:
```python
import jax
import jax.numpy as jnp
from jax import lax
from jax.experimental import pallas as pl
from jax.experimental.pallas import tpu as pltpu
from jax.sharding import PartitionSpec as P

MESH = pl.DeviceIdType.MESH
EPS = 1e-06
N = 1500
NP = 1536
LAST = N - 11 * 128
ZC = NP // 8
F32, BF16 = jnp.float32, jnp.bfloat16
MESSAGES = 192


def dot(a, b):
    return lax.dot_general(a, b, (((1,), (0,)), ((), ())), preferred_element_type=F32)


def turn(x):
    lane = lax.broadcasted_iota(jnp.int32, x.shape, 1)
    rolled = pltpu.roll(x, 64, 1)
    return jnp.where(lane < 64, -rolled, rolled)


def tile_sum(x):
    rows, cols = x.shape
    total = None
    for j in range(cols // 128):
        part = jnp.sum(x[:, 128 * j : 128 * j + 128].reshape(rows // 8, 8, 128), axis=0)
        total = part if total is None else total + part
    return total


def full_sum(tile):
    return jnp.sum(jnp.sum(tile, axis=0, keepdims=True), axis=1, keepdims=True)


def kernel(op_hbm, rec, sol, res, en, tail, xs, xc, u, wt, z, pb, fb, pf, ff, rzh, rzf, ryc, ryh, ryf,
           sbuf, rrow, rcol, rfreq, load_sem, send_sem, recv_sem):
    freq, row, col = lax.axis_index("freq"), lax.axis_index("row"), lax.axis_index("col")
    y, q = row // 2, row % 2

    source = op_hbm.reshape(2 * N, N)
    loads = [
        pltpu.make_async_copy(source.at[:, pl.ds(128 * j, 128)], en.at[j, pl.ds(0, 2 * N)], load_sem.at[j])
        for j in range(11)
    ]
    loads.append(pltpu.make_async_copy(source.at[:, pl.ds(1408, LAST)], tail, load_sem.at[11]))
    for c in loads:
        c.start()

    row_peers = [{"row": (row + k) % 8} for k in range(1, 8)]
    col_peers = [{"col": (col + k) % 8} for k in range(1, 8)]
    freq_peers = [{"freq": (freq + k) % 4} for k in range(1, 4)]
    barrier = pltpu.get_barrier_semaphore()
    for peer in row_peers + col_peers + freq_peers:
        pl.semaphore_signal(barrier, inc=1, device_id=peer, device_id_type=MESH)

    count = [0]
    sent = []

    def message(src, dst, peer):
        k = count[0]
        count[0] += 1
        copy = pltpu.make_async_remote_copy(
            src_ref=src, dst_ref=dst, send_sem=send_sem.at[k], recv_sem=recv_sem.at[k],
            device_id=peer, device_id_type=MESH)
        copy.start()
        sent.append(copy)
        return k

    def arrive(k, dst):
        pltpu.make_async_remote_copy(
            src_ref=dst, dst_ref=dst, send_sem=send_sem.at[k], recv_sem=recv_sem.at[k],
            device_id={"col": (col + 1) % 8}, device_id_type=MESH).wait_recv()

    def zrows(k, part=None):
        start = pl.multiple_of(ZC * ((col + k + 8) % 8), 64)
        if part is None:
            return pl.ds(start, ZC)
        return pl.ds(pl.multiple_of(start + part * (ZC // 2), 32), ZC // 2)

    z_up, z_down = {"col": (col + 1) % 8}, {"col": (col + 7) % 8}

    def z_phase(it, s):
        p, f = pf.at[it, s], ff.at[it, s]
        half, full = rzh.at[it, s], rzf.at[it, s]
        a = message(p.at[zrows(4, 0)], half.at[0], z_up)
        b = message(p.at[zrows(4, 1)], half.at[1], z_down)
        yield
        arrive(a, half.at[0])
        p[zrows(3, 0), :] += half[0]
        a = message(p.at[zrows(3)], full.at[0, 0], z_up)
        arrive(b, half.at[1])
        p[zrows(-3, 1), :] += half[1]
        b = message(p.at[zrows(-3)], full.at[1, 0], z_down)
        yield
        for step in range(2):
            arrive(a, full.at[0, step])
            p[zrows(2 - step), :] += full[0, step]
            a = message(p.at[zrows(2 - step)], full.at[0, step + 1], z_up)
            arrive(b, full.at[1, step])
            p[zrows(step - 2), :] += full[1, step]
            b = message(p.at[zrows(step - 2)], full.at[1, step + 1], z_down)
            yield
        arrive(a, full.at[0, 2])
        arrive(b, full.at[1, 2])
        f[zrows(0), :] = p[zrows(0), :] + full[0, 2] + full[1, 2]
        a = message(f.at[zrows(0)], f.at[zrows(0)], z_up)
        b = message(f.at[zrows(0)], f.at[zrows(0)], z_down)
        yield
        for step in range(1, 3):
            arrive(a, f.at[zrows(-step)])
            a = message(f.at[zrows(-step)], f.at[zrows(-step)], z_up)
            arrive(b, f.at[zrows(step)])
            b = message(f.at[zrows(step)], f.at[zrows(step)], z_down)
            yield
        arrive(a, f.at[zrows(-3)])
        a = message(f.at[zrows(-3, 0)], f.at[zrows(-3, 0)], z_up)
        arrive(b, f.at[zrows(3)])
        b = message(f.at[zrows(3, 1)], f.at[zrows(3, 1)], z_down)
        yield
        arrive(a, f.at[zrows(4, 0)])
        arrive(b, f.at[zrows(4, 1)])
        yield

    def yrows(k, part=None, core=None):
        owner = 4 * (q if core is None else core) + (y + k + 4) % 4
        start = pl.multiple_of(16 * owner, 16)
        if part is None:
            return pl.ds(start, 16)
        return pl.ds(pl.multiple_of(start + 8 * part, 8), 8)

    y_up, y_down = {"row": 2 * ((y + 1) % 4) + q}, {"row": 2 * ((y + 3) % 4) + q}
    twin = {"row": 2 * y + (1 - q)}
    mine, other = pl.ds(pl.multiple_of(64 * q, 64), 64), pl.ds(pl.multiple_of(64 * (1 - q), 64), 64)

    def y_phase(it, s):
        p, f = pb.at[it, s], fb.at[it, s]
        half, full = ryh.at[it, s], ryf.at[it, s]
        a = message(p.at[other], ryc.at[it, s], twin)
        yield
        arrive(a, ryc.at[it, s])
        p[mine, :] += ryc[it, s]
        a = message(p.at[yrows(2, 0)], half.at[0], y_up)
        b = message(p.at[yrows(2, 1)], half.at[1], y_down)
        yield
        arrive(a, half.at[0])
        p[yrows(1, 0), :] += half[0]
        a = message(p.at[yrows(1)], full.at[0], y_up)
        arrive(b, half.at[1])
        p[yrows(-1, 1), :] += half[1]
        b = message(p.at[yrows(-1)], full.at[1], y_down)
        yield
        arrive(a, full.at[0])
        arrive(b, full.at[1])
        f[yrows(0), :] = p[yrows(0), :] + full[0] + full[1]
        a = message(f.at[yrows(0)], f.at[yrows(0)], y_up)
        b = message(f.at[yrows(0)], f.at[yrows(0)], y_down)
        twins = [(message(f.at[yrows(0)], f.at[yrows(0)], twin), 0)]
        yield
        arrive(a, f.at[yrows(-1)])
        a = message(f.at[yrows(-1, 0)], f.at[yrows(-1, 0)], y_up)
        twins.append((message(f.at[yrows(-1)], f.at[yrows(-1)], twin), -1))
        arrive(b, f.at[yrows(1)])
        b = message(f.at[yrows(1, 1)], f.at[yrows(1, 1)], y_down)
        twins.append((message(f.at[yrows(1)], f.at[yrows(1)], twin), 1))
        yield
        arrive(a, f.at[yrows(2, 0)])
        arrive(b, f.at[yrows(2, 1)])
        twins.append((message(f.at[yrows(2)], f.at[yrows(2)], twin), 2))
        yield
        for k, place in twins:
            arrive(k, f.at[yrows(place, core=1 - q)])
        yield

    def exchange(n, tiles, out):
        rows = 8 * len(tiles)
        value = jnp.concatenate(tiles, axis=0) if len(tiles) > 1 else tiles[0]
        for stage, (slots, size, me, peers) in enumerate(
            ((rrow, 8, row, row_peers), (rcol, 8, col, col_peers), (rfreq, 4, freq, freq_peers))
        ):
            sbuf[n, stage, pl.ds(0, rows), :] = value
            slots[n, me, pl.ds(0, rows), :] = value
            keys = [
                message(sbuf.at[n, stage, pl.ds(0, rows)], slots.at[n, me, pl.ds(0, rows)], peer) for peer in peers
            ]
            yield
            for k, key in enumerate(keys):
                arrive(key, slots.at[n, (me + size - k - 1) % size, pl.ds(0, rows)])
            value = slots[n, 0, pl.ds(0, rows), :]
            for j in range(1, size):
                value = value + slots[n, j, pl.ds(0, rows), :]
        out.extend(full_sum(value[8 * i : 8 * i + 8]) for i in range(len(tiles)))
        yield

    def set_weights(s, value):
        xs[pl.ds(0, NP, 2), :] = value
        xs[pl.ds(1, NP, 2), :] = -turn(value)
        for b in range(24):
            wt[s, :, 128 * b : 128 * b + 128] = xs[128 * b : 128 * b + 128, :].T.astype(BF16)

    def adjoint(it, s, lo, hi):
        @pl.loop(lo, hi)
        def _(j):
            block = jnp.concatenate([en[2 * j], en[2 * j + 1]], axis=1)
            pb[it, s, :, pl.ds(pl.multiple_of(256 * j, 256), 256)] = dot(wt[s], block)

    def forward_chunk(it, s, k):
        c = (col + k) % 8
        rows = pl.ds(pl.multiple_of(2 * ZC * c, 128), 2 * ZC)
        xc[...] = dot(jnp.concatenate([en[j, rows, :] for j in range(12)], axis=1), z[s])
        pf[it, s, pl.ds(pl.multiple_of(ZC * c, 64), ZC), :] = xc[pl.ds(0, ZC, 2), :] + turn(xc[pl.ds(1, ZC, 2), :])

    def forward(it, s):
        forward_chunk(it, s, 4)
        yield
        for first, step in ((3, 2), (2, 4), (1, 6)):
            @pl.loop(0, 2)
            def _(i):
                forward_chunk(it, s, first + step * i)
            yield
        forward_chunk(it, s, 0)
        yield

    def own_z(ref, it, s):
        return ref[it, s, zrows(0), :]

    xs[pl.ds(0, 2 * N), :] = rec[...].astype(F32)
    xs[pl.ds(2 * N, 72), :] = jnp.zeros((72, 128), F32)
    lane = lax.broadcasted_iota(jnp.int32, (NP, 128), 1)
    re, im = xs[pl.ds(0, NP, 2), :], xs[pl.ds(1, NP, 2), :]
    u[0] = jnp.where(lane < 64, re, pltpu.roll(im, 64, 1))
    u[1] = jnp.where(lane < 64, pltpu.roll(re, 64, 1), im)
    set_weights(0, u[0])
    set_weights(1, u[1])
    own_u = [u[s, zrows(0), :] for s in range(2)]
    beta1_tile = tile_sum(own_u[0] * own_u[0]) + tile_sum(own_u[1] * own_u[1])
    for c in loads:
        c.wait()
    en[:, pl.ds(2 * N, 72), :] = jnp.zeros((12, 72, 128), BF16)
    en[11] = jnp.pad(tail[...], ((0, 72), (0, 128 - LAST)))

    adjoint(0, 0, 0, 6)
    pl.semaphore_wait(barrier, len(row_peers + col_peers + freq_peers))

    ra, rb = y_phase(0, 0), y_phase(0, 1)
    next(ra)
    adjoint(0, 1, 0, 6)
    next(ra)
    next(rb)
    next(ra)
    next(rb)
    next(ra)
    next(rb)
    next(ra)
    next(rb)
    own = [fb[0, s, yrows(0), :] for s in range(2)]
    norms = []
    x0 = exchange(0, [beta1_tile, tile_sum(own[0] * own[0]) + tile_sum(own[1] * own[1])], norms)
    next(x0)
    next(ra)
    next(rb)
    next(ra)

    def set_operand(s, value):
        for b in range(12):
            z[s, 128 * b : 128 * b + 128, :] = value(b).T.astype(BF16)

    def lanes(b):
        return pl.ds(128 * b, 128)

    set_operand(0, lambda b: fb[0, 0, :, lanes(b)])
    ma, za = forward(0, 0), z_phase(0, 0)
    next(ma)
    next(za)
    next(rb)
    next(ma)
    next(za)
    next(rb)
    next(x0)
    next(ma)
    next(za)
    set_operand(1, lambda b: fb[0, 1, :, lanes(b)])
    next(ma)
    next(za)
    next(x0)
    next(ma)
    mb, zb = forward(0, 1), z_phase(0, 1)
    next(mb)
    next(zb)
    next(za)
    next(mb)
    next(zb)
    next(za)
    next(x0)
    beta1 = jnp.sqrt(norms[0] + EPS)
    alpha1 = jnp.sqrt(norms[1] / (beta1 * beta1) + EPS)
    k1 = 1.0 / (beta1 * alpha1)
    k2 = alpha1 / beta1
    next(mb)
    next(zb)
    next(za)
    next(mb)
    next(zb)
    next(za)
    next(mb)
    next(za)

    def update(s):
        return ff[0, s] * k1 - u[s] * k2

    set_weights(0, update(0))
    next(zb)
    own_update = [own_z(ff, 0, s) * k1 - own_u[s] * k2 for s in range(2)]
    x1 = exchange(1, [tile_sum(own_update[0] * own_update[0]) + tile_sum(own_update[1] * own_update[1])], norms)
    next(x1)
    adjoint(1, 0, 0, 3)
    next(zb)
    adjoint(1, 0, 3, 6)
    ra, rb = y_phase(1, 0), y_phase(1, 1)
    next(ra)
    next(zb)
    next(ra)
    next(x1)
    next(zb)
    next(ra)
    next(x1)
    next(zb)
    set_weights(1, update(1))
    next(ra)
    adjoint(1, 1, 0, 3)
    next(ra)
    adjoint(1, 1, 3, 6)
    next(rb)
    next(x1)
    beta2 = jnp.sqrt(norms[2] + EPS)
    ib2 = 1.0 / beta2
    k3 = beta2 * k1
    next(ra)
    next(rb)
    next(ra)
    set_operand(0, lambda b: fb[1, 0, :, lanes(b)] * ib2 - fb[0, 0, :, lanes(b)] * k3)
    ma, za = forward(1, 0), z_phase(1, 0)
    next(ma)
    next(za)
    next(rb)
    next(ma)
    next(za)
    next(rb)
    own = [fb[1, s, yrows(0), :] * ib2 - fb[0, s, yrows(0), :] * k3 for s in range(2)]
    x2 = exchange(2, [tile_sum(own[0] * own[0]) + tile_sum(own[1] * own[1])], norms)
    next(x2)
    next(ma)
    next(za)
    next(rb)
    next(ma)
    next(za)
    next(rb)
    next(x2)
    next(ma)
    next(rb)
    set_operand(1, lambda b: fb[1, 1, :, lanes(b)] * ib2 - fb[0, 1, :, lanes(b)] * k3)
    mb, zb = forward(1, 1), z_phase(1, 1)
    next(mb)
    next(zb)
    next(za)
    next(x2)
    next(mb)
    next(zb)
    next(za)
    next(x2)
    alpha2 = jnp.sqrt(norms[3] + EPS)
    ia2 = 1.0 / alpha2
    next(mb)
    next(zb)
    next(za)
    next(mb)
    next(zb)
    next(za)
    next(mb)
    next(za)
    next(zb)
    own_last = [own_z(ff, 1, s) * ia2 - own_update[s] * (alpha2 * ib2) for s in range(2)]
    x3 = exchange(3, [tile_sum(own_last[0] * own_last[0]) + tile_sum(own_last[1] * own_last[1])], norms)
    next(x3)
    next(zb)
    next(x3)
    next(zb)
    next(x3)
    next(zb)
    next(x3)
    beta3 = jnp.sqrt(norms[4] + EPS)
    rho1 = jnp.sqrt(alpha1 * alpha1 + beta2 * beta2)
    cos1, sin1 = alpha1 / rho1, beta2 / rho1
    gain1 = cos1 * beta1 / rho1
    ratio = sin1 * alpha2 / rho1
    rho_bar = -cos1 * alpha2
    rho2 = jnp.sqrt(rho_bar * rho_bar + beta3 * beta3)
    gain2 = rho_bar / rho2 * (sin1 * beta1) / rho2
    first, second = (gain1 - gain2 * ratio) * k1, gain2 * ia2
    second_a, second_b = second * ib2, first - second * k3

    for part in range(2):
        for b in range(12):
            rows = pl.ds(64 * part, 64)
            block = jnp.concatenate(
                [fb[1, s, rows, lanes(b)] * second_a + fb[0, s, rows, lanes(b)] * second_b for s in range(2)], axis=0)
            size = 128 if b < 11 else LAST
            sol[pl.ds(256 * b + part, size, 2), :] = block.T[:size]
    next(zb)
    lane = lax.broadcasted_iota(jnp.int32, (N, 128), 1)
    out = [
        u[s, pl.ds(0, N), :] - ff[0, s, pl.ds(0, N), :] * first - ff[1, s, pl.ds(0, N), :] * second for s in range(2)
    ]
    res[pl.ds(0, N, 2), :] = jnp.where(lane < 64, out[0], pltpu.roll(out[1], 64, 1))
    res[pl.ds(1, N, 2), :] = jnp.where(lane < 64, pltpu.roll(out[0], 64, 1), out[1])

    for copy in sent:
        copy.wait_send()


def shards(operator, recorded):
    op = jnp.transpose(operator[0], (1, 0, 2))
    rec = jnp.transpose(recorded[0], (1, 0, 2)).reshape(2 * N, 128)
    vmem = pl.BlockSpec(memory_space=pltpu.VMEM)
    out = jax.ShapeDtypeStruct((2 * N, 128), F32)
    sol, res = pl.pallas_call(
        kernel,
        out_shape=[out, out],
        in_specs=[pl.BlockSpec(memory_space=pl.ANY), vmem],
        out_specs=[vmem, vmem],
        scratch_shapes=[
            pltpu.VMEM((12, 2 * NP, 128), BF16),
            pltpu.VMEM((2 * N, LAST), BF16),
            pltpu.VMEM((2 * NP, 128), F32),
            pltpu.VMEM((2 * ZC, 128), F32),
            pltpu.VMEM((2, NP, 128), F32),
            pltpu.VMEM((2, 128, 2 * NP), BF16),
            pltpu.VMEM((2, NP, 128), BF16),
            pltpu.VMEM((2, 2, 128, NP), F32),
            pltpu.VMEM((2, 2, 128, NP), F32),
            pltpu.VMEM((2, 2, NP, 128), F32),
            pltpu.VMEM((2, 2, NP, 128), F32),
            pltpu.VMEM((2, 2, 2, ZC // 2, 128), F32),
            pltpu.VMEM((2, 2, 2, 3, ZC, 128), F32),
            pltpu.VMEM((2, 2, 64, NP), F32),
            pltpu.VMEM((2, 2, 2, 8, NP), F32),
            pltpu.VMEM((2, 2, 2, 16, NP), F32),
            pltpu.VMEM((4, 3, 16, 128), F32),
            pltpu.VMEM((4, 8, 16, 128), F32),
            pltpu.VMEM((4, 8, 16, 128), F32),
            pltpu.VMEM((4, 4, 16, 128), F32),
            pltpu.SemaphoreType.DMA((12,)),
            pltpu.SemaphoreType.DMA((MESSAGES,)),
            pltpu.SemaphoreType.DMA((MESSAGES,)),
        ],
        compiler_params=pltpu.CompilerParams(
            collective_id=0, has_side_effects=True, vmem_limit_bytes=60 * 2**20),
        cost_estimate=pl.CostEstimate(flops=9_437_184_000, bytes_accessed=13_000_000, transcendentals=0),
    )(op, rec)
    return tuple(jnp.transpose(o.reshape(N, 2, 128), (1, 0, 2))[None] for o in (sol, res))


def solution(mesh):
    in_specs = (P("freq", None, "row", "col"), P("freq", None, "row", None))
    out_specs = (P("freq", None, "col", None), P("freq", None, "row", None))
    return jax.shard_map(shards, mesh=mesh, in_specs=in_specs, out_specs=out_specs, check_vma=False)
```

time: 722 us -> 159 us (0.22)
  blocking collectives: 324 us -> 0 us
  waiting for transfers between devices: 294 us -> 0 us
  Pallas kernels: 0 us -> 153 us
  local copies, waits for them, and re-layouts: 36.7 us -> 3.56 us
  matrix products: 27.7 us -> 0 us
  other arithmetic: 20.9 us -> 0 us
  between operations: 17.7 us -> 0.65 us
    psum x5 -> x0, blocking collectives: 324 us -> none  [the longest x2 135 us: forward_reduce(): squares = lax.psum(jnp.sum(update * update), ('freq', 'row'))]
    psum x4 -> x0, waiting for transfers between devices: 294 us -> none  [the longest x2 165 us: forward_reduce(): imaged = lax.psum(partial_value, 'col')]
    pallas_call x0 -> x1, Pallas kernels: none -> 153 us  [shards(): pl.pallas_call(kernel, out_shape=[out, out], in_specs=[pl.BlockSpec(memor...]
    dot_general x4 -> x0, matrix products: 27.7 us -> none  [the longest x2 14.5 us: adjoint_part(): jnp.einsum('krc,lrs->klcs', operator[0], vector[0], preferred_element_typ...]
    squeeze x1 -> x0, local copies, waits for them, and re-layouts: 23.8 us -> none  [adjoint_part(): operator[0]]
    reduce_sum x5 -> x0, other arithmetic: 12.4 us -> none  [the longest x2 5.36 us: forward_reduce(): squares = lax.psum(jnp.sum(update * update), ('freq', 'row'))]
    unnamed x8 -> x4, local copies, waits for them, and re-layouts: 12.9 us -> 3.56 us
  transfers between devices with their start and end apart: 4 -> 0, of which waited for: 4 -> 0; matrix products, arithmetic and copies ran while one was open for 0% -> 0% of each run, Pallas kernels for 0% -> 0%
where the time goes in v1:
time: 159 us; the launch traced here: 157 us
  Pallas kernels  153 us (96%)
  local copies, waits for them, and re-layouts  3.56 us (2%)
    pallas_call x1, Pallas kernels, shards(): pl.pallas_call(kernel, out_shape=[out, out], in_specs=[pl.BlockSpec(memor...  153 us
    unnamed x4, local copies, waits for them, and re-layouts  3.56 us

profile of v1, /device:TPU:1, one launch (start us, length us, event | category | flops | bytes accessed | tf_op | source)
XLA Modules:
  0.0 156.9 jit_solution(10819708090546379470)
XLA Ops:
  0.6 152.7 %shard_map.41 = (f32[3000,128]{1,0:T(8,128)}, f32[3000,128]{1,0:T(8,128)}) custom-call(bf16[1500,2,1500]{2,1,0:T(2,128)(2,1)} %bitcast.20, bf16[3000,128]{1,0:T(8,128)(2,1)} %bitcast.21), custom_call_target="tpu_custom_call" | custom-call | flops 9437184000 | bytes 13000000 | tf_op jit(solution)/shard_map/pallas_call | solution.py:431
  153.4 0.0 copy-start
  153.4 2.4 %copy.6 = f32[1,2,1500,128]{3,1,2,0:T(2,128)} copy(f32[1,2,1500,128]{3,1,2,0:T(2,128)} %bitcast.19) | data formatting | bytes 3072000
  155.8 0.0 copy-done
  155.8 1.1 copy.7
Async XLA Ops:
  153.4 2.4 %copy-start = (f32[3000,128]{1,0:T(8,128)S(1)}, f32[3000,128]{1,0:T(8,128)}, u32[]{:S(2)}) copy-start(f32[3000,128]{1,0:T(8,128)} %get-tuple-element.5) | copy-start | bytes 4608004

commit v2 on v0

v2 whole, which is shorter than its diff:
```python
import math

import jax
import jax.numpy as jnp
from jax import lax
from jax.experimental import pallas as pl
from jax.experimental.pallas import tpu as pltpu
from jax.sharding import PartitionSpec as P

MESH = pl.DeviceIdType.MESH
EPS = 1e-06
N = 1500
NP = 1536
LAST = N - 11 * 128
ZC = NP // 8
F32, BF16 = jnp.float32, jnp.bfloat16
MESSAGES = 304
SUBS = 2
Y_SUBS = 2
Y_DIRECT = False
LAT = 2.3
RS_SHORT = False
AG_SHORT = False


def dot(a, b):
    return lax.dot_general(a, b, (((1,), (0,)), ((), ())), preferred_element_type=F32)


def turn(x):
    lane = lax.broadcasted_iota(jnp.int32, x.shape, 1)
    rolled = pltpu.roll(x, 64, 1)
    return jnp.where(lane < 64, -rolled, rolled)


def tile_sum(x):
    rows, cols = x.shape
    total = None
    for j in range(cols // 128):
        part = jnp.sum(x[:, 128 * j : 128 * j + 128].reshape(rows // 8, 8, 128), axis=0)
        total = part if total is None else total + part
    return total


def full_sum(tile):
    return jnp.sum(jnp.sum(tile, axis=0, keepdims=True), axis=1, keepdims=True)


class Plan:
    def __init__(self):
        self.now, self.links, self.due, self.marks = 0.0, {}, [], set()

    def send(self, links, occupied, latency):
        self.now += 0.05
        start = max([self.now] + [self.links.get(link, 0.0) for link in links])
        for link in links:
            self.links[link] = start + occupied
        self.due.append(start + occupied + latency)
        return len(self.due) - 1

    def run(self, streams):
        waiting = [(stream, next(stream)) for stream in streams]
        while waiting:
            best = None
            for place, (stream, (keys, marks)) in enumerate(waiting):
                if all(mark in self.marks for mark in marks):
                    ready = max([self.now] + [self.due[k] for k in keys])
                    if best is None or ready < best[0]:
                        best = (ready, place)
            self.now, place = best
            stream = waiting[place][0]
            try:
                waiting[place] = (stream, next(stream))
            except StopIteration:
                del waiting[place]


def kernel(op_hbm, rec, sol, res, en, tail, xs, xc, u, wt, z, pb, fb, pf, ff, rzh, rzf, ryc, ryh, ryf,
           sbuf, rrow, rcol, rfreq, load_sem, send_sem, recv_sem):
    freq, row, col = lax.axis_index("freq"), lax.axis_index("row"), lax.axis_index("col")
    y, q = row // 2, row % 2
    plan = Plan()

    source = op_hbm.reshape(2 * N, N)
    loads = [
        pltpu.make_async_copy(source.at[:, pl.ds(128 * j, 128)], en.at[j, pl.ds(0, 2 * N)], load_sem.at[j])
        for j in range(11)
    ]
    loads.append(pltpu.make_async_copy(source.at[:, pl.ds(1408, LAST)], tail, load_sem.at[11]))
    for c in loads:
        c.start()

    row_peers = [{"row": (row + k) % 8} for k in range(1, 8)]
    col_peers = [{"col": (col + k) % 8} for k in range(1, 8)]
    freq_peers = [{"freq": (freq + k) % 4} for k in range(1, 4)]
    peers = row_peers + col_peers + freq_peers
    barrier = pltpu.get_barrier_semaphore()
    for peer in peers:
        pl.semaphore_signal(barrier, inc=1, device_id=peer, device_id_type=MESH)

    sent = []

    def message(src, dst, peer, links=(), hops=1, latency=LAT):
        if not sent:
            pl.semaphore_wait(barrier, len(peers))
        size = 4 * math.prod(src.shape)
        k = plan.send(links, hops * size * 2e-5 if links else size * 1.5e-6, latency + 0.6 * (hops - 1))
        copy = pltpu.make_async_remote_copy(
            src_ref=src, dst_ref=dst, send_sem=send_sem.at[k], recv_sem=recv_sem.at[k],
            device_id=peer, device_id_type=MESH)
        copy.start()
        sent.append(copy)
        return k

    def arrive(k, dst):
        pltpu.make_async_remote_copy(
            src_ref=dst, dst_ref=dst, send_sem=send_sem.at[k], recv_sem=recv_sem.at[k],
            device_id={"col": (col + 1) % 8}, device_id_type=MESH).wait_recv()

    def mark(*name):
        plan.marks.add(name)

    size = ZC // SUBS

    def zrows(k, h, part=None):
        start = ZC * ((col + k + 8) % 8) + size * h
        if part is None:
            return pl.ds(pl.multiple_of(start, 16), size)
        return pl.ds(pl.multiple_of(start + part * (size // 2), 16), size // 2)

    def z_peer(step):
        return {"col": (col + 8 + step) % 8}

    def z_phase(it, s, h):
        p, f = pf.at[it, s], ff.at[it, s]
        half, full = rzh.at[it, s, h], rzf.at[it, s, h]
        signs = (1, -1)

        def go(src, dst, sign, hops=1):
            return message(src, dst, z_peer(sign * hops), (("z", sign),), hops)

        yield [], [("pf", it, s, 0)]
        if RS_SHORT:
            far = [go(p.at[zrows(4, h, d)], half.at[d], sign, 2) for d, sign in enumerate(signs)]
        else:
            far = [go(p.at[zrows(4, h, d)], half.at[d], sign) for d, sign in enumerate(signs)]
        keys = [None, None]
        for step in (3, 2, 1):
            for d, sign in enumerate(signs):
                at = 2 if RS_SHORT else 3
                needs = ([] if step == 3 else [keys[d]]) + ([far[d]] if step == at else [])
                yield needs, [("pf", it, s, 4 - step)]
                if step < 3:
                    arrive(keys[d], full.at[d, 2 - step])
                    p[zrows(sign * step, h), :] += full[d, 2 - step]
                if step == at:
                    arrive(far[d], half.at[d])
                    p[zrows(sign * step, h, d), :] += half[d]
                keys[d] = go(p.at[zrows(sign * step, h)], full.at[d, 3 - step], sign)
        yield keys, [("pf", it, s, 4)]
        for d in range(2):
            arrive(keys[d], full.at[d, 2])
        f[zrows(0, h), :] = p[zrows(0, h), :] + full[0, 2] + full[1, 2]
        mark("own_z", it, s, h)
        here = f.at[zrows(0, h)]
        keys = [go(here, here, sign) for sign in signs]
        for step in (1, 2, 3):
            for d, sign in enumerate(signs):
                yield [keys[d]], []
                block = f.at[zrows(-sign * step, h)]
                arrive(keys[d], block)
                if step == 2 and AG_SHORT:
                    part = f.at[zrows(-sign * step, h, d)]
                    far[d] = go(part, part, sign, 2)
                if step < 3:
                    keys[d] = go(block, block, sign)
                elif not AG_SHORT:
                    part = f.at[zrows(-sign * step, h, d)]
                    far[d] = go(part, part, sign)
        yield far, []
        for d in range(2):
            arrive(far[d], f.at[zrows(4, h, d)])
        mark("ff", it, s, h)

    def yrows(k, core=None, part=None):
        owner = 4 * (q if core is None else core) + (y + k + 4) % 4
        if part is None:
            return pl.ds(pl.multiple_of(16 * owner, 16), 16)
        return pl.ds(pl.multiple_of(16 * owner + 8 * part, 8), 8)

    y_links = {1: (("y", 1),), 2: (("y", 1), ("y", -1)), 3: (("y", -1),)}
    twin = {"row": 2 * y + (1 - q)}
    mine, other = pl.ds(pl.multiple_of(64 * q, 64), 64), pl.ds(pl.multiple_of(64 * (1 - q), 64), 64)
    width = NP // Y_SUBS

    def y_phase(it, s, h):
        across = pl.ds(width * h, width)
        p, f = pb.at[it, s], fb.at[it, s]
        core_half, half, full = ryc.at[it, s, h], ryh.at[it, s, h], ryf.at[it, s, h]
        signs = (1, -1)

        def go(src, dst, k):
            return message(src, dst, {"row": 2 * ((y + k) % 4) + q}, y_links[k], 1, LAT + (0.6 if k == 2 else 0.0))

        def pass_on(k):
            block = f.at[yrows(k), across]
            return message(block, block, twin, (), 1, 0.9), k

        yield [], [("pb", it, s, part) for part in range(3) if 512 * part < width * (h + 1)]
        a = message(p.at[other, across], core_half, twin, (), 1, 0.9)
        yield [a], []
        arrive(a, core_half)
        p[mine, across] += core_half[...]
        if Y_DIRECT:
            keys = {k: go(p.at[yrows(k), across], full.at[k - 1], k) for k in (2, 1, 3)}
            yield list(keys.values()), []
            total = p[yrows(0), across]
            for k in (1, 3, 2):
                arrive(keys[k], full.at[k - 1])
                total = total + full[k - 1]
        else:
            far = [go(p.at[yrows(2, None, d), across], half.at[d], sign % 4) for d, sign in enumerate(signs)]
            keys = [None, None]
            for d, sign in enumerate(signs):
                yield [far[d]], []
                arrive(far[d], half.at[d])
                p[yrows(sign, None, d), across] += half[d]
                keys[d] = go(p.at[yrows(sign), across], full.at[d], sign % 4)
            yield keys, []
            total = p[yrows(0), across]
            for d in range(2):
                arrive(keys[d], full.at[d])
                total = total + full[d]
        f[yrows(0), across] = total
        mark("own_y", it, s, h)
        here = f.at[yrows(0), across]
        if Y_DIRECT:
            keys = {k: go(here, here, k) for k in (2, 1, 3)}
            twins = [pass_on(0)]
            for k in (1, 3, 2):
                yield [keys[k]], []
                arrive(keys[k], f.at[yrows(-k), across])
                twins.append(pass_on(-k))
        else:
            keys = [go(here, here, sign % 4) for sign in signs]
            twins = [pass_on(0)]
            for d, sign in enumerate(signs):
                yield [keys[d]], []
                arrive(keys[d], f.at[yrows(-sign), across])
                part = f.at[yrows(-sign, None, d), across]
                far[d] = go(part, part, sign % 4)
                twins.append(pass_on(-sign))
            yield far, []
            for d in range(2):
                arrive(far[d], f.at[yrows(2, None, d), across])
            twins.append(pass_on(2))
        yield [k for k, _ in twins], []
        for k, place in twins:
            arrive(k, f.at[yrows(place, core=1 - q), across])
        mark("fb", it, s, h)

    norms = {}

    def exchange(n, names, needs, tiles):
        yield [], needs
        value = tiles()
        rows = 8 * len(names)
        for stage, (slots, size, me, group, hops) in enumerate(
            ((rrow, 8, row, row_peers, 2), (rcol, 8, col, col_peers, 4), (rfreq, 4, freq, freq_peers, 2))
        ):
            sbuf[n, stage, pl.ds(0, rows), :] = value
            slots[n, me, pl.ds(0, rows), :] = value
            order = sorted(range(size - 1), key=lambda k: abs(2 * k + 2 - size))
            keys = {
                k: message(sbuf.at[n, stage, pl.ds(0, rows)], slots.at[n, me, pl.ds(0, rows)], group[k], (), hops)
                for k in order
            }
            yield list(keys.values()), []
            for k, key in keys.items():
                arrive(key, slots.at[n, (me + size - k - 1) % size, pl.ds(0, rows)])
            value = slots[n, 0, pl.ds(0, rows), :]
            for j in range(1, size):
                value = value + slots[n, j, pl.ds(0, rows), :]
        for i, name in enumerate(names):
            norms[name] = full_sum(value[8 * i : 8 * i + 8])
        mark("x", n)

    def lanes(b):
        return pl.ds(128 * b, 128)

    def set_weights(s, value):
        xs[pl.ds(0, NP, 2), :] = value
        xs[pl.ds(1, NP, 2), :] = -turn(value)
        for b in range(24):
            wt[s, :, 128 * b : 128 * b + 128] = xs[128 * b : 128 * b + 128, :].T.astype(BF16)
        plan.now += 0.4

    loaded = []

    def fetched(part):
        for j in range(4 * part, 4 * part + 4):
            loads[j].wait()
            if j < 11:
                en[j, pl.ds(2 * N, 72), :] = jnp.zeros((72, 128), BF16)
            else:
                en[11] = jnp.pad(tail[...], ((0, 72), (0, 128 - LAST)))
        loaded.append(part)

    def adjoint(it, s):
        for part in range(3):
            yield [], []
            if part not in loaded:
                fetched(part)
            block = jnp.concatenate([en[4 * part + j] for j in range(4)], axis=1)
            pb[it, s, :, 512 * part : 512 * part + 512] = dot(wt[s], block)
            plan.now += 0.5
            mark("pb", it, s, part)

    def set_operand(s, value):
        for b in range(12):
            z[s, 128 * b : 128 * b + 128, :] = value(b).T.astype(BF16)
        plan.now += 0.2

    def forward_chunk(it, s, k, i):
        c = (col + k) % 8
        rows = pl.ds(pl.multiple_of(2 * ZC * c, 128), 2 * ZC)
        xc[i] = dot(jnp.concatenate([en[j, rows, :] for j in range(12)], axis=1), z[s])
        even, odd = xc[i, pl.ds(0, ZC, 2), :], xc[i, pl.ds(1, ZC, 2), :]
        pf[it, s, pl.ds(pl.multiple_of(ZC * c, 64), ZC), :] = even + turn(odd)

    def forward(it, s):
        for group, (first, step, count) in enumerate(((4, 0, 1), (3, 2, 2), (2, 4, 2), (1, 6, 2), (0, 0, 1))):
            yield [], []
            for i in range(count):
                forward_chunk(it, s, first + step * i, i)
            plan.now += 0.4 * count
            mark("pf", it, s, group)

    xs[pl.ds(0, 2 * N), :] = rec[...].astype(F32)
    xs[pl.ds(2 * N, 72), :] = jnp.zeros((72, 128), F32)
    lane = lax.broadcasted_iota(jnp.int32, (NP, 128), 1)
    re, im = xs[pl.ds(0, NP, 2), :], xs[pl.ds(1, NP, 2), :]
    u[0] = jnp.where(lane < 64, re, pltpu.roll(im, 64, 1))
    u[1] = jnp.where(lane < 64, pltpu.roll(re, 64, 1), im)
    set_weights(0, u[0])
    set_weights(1, u[1])

    def own_rows(ref):
        return ref[pl.ds(pl.multiple_of(ZC * col, 64), ZC), :]

    def square_sum(values):
        return tile_sum(values[0] * values[0]) + tile_sum(values[1] * values[1])

    val = {}

    def tiles0():
        own = [fb[0, s, yrows(0), :] for s in range(2)]
        return jnp.concatenate([square_sum([own_rows(u.at[s]) for s in range(2)]), square_sum(own)], axis=0)

    def after0():
        if "k1" not in val:
            val["beta1"] = jnp.sqrt(norms["beta1"] + EPS)
            val["alpha1"] = jnp.sqrt(norms["alpha1"] / (val["beta1"] * val["beta1"]) + EPS)
            val["k1"] = 1.0 / (val["beta1"] * val["alpha1"])
            val["k2"] = val["alpha1"] / val["beta1"]

    def own_update(s):
        after0()
        return own_rows(ff.at[0, s]) * val["k1"] - own_rows(u.at[s]) * val["k2"]

    def tiles1():
        return square_sum([own_update(s) for s in range(2)])

    def after1():
        if "ib2" not in val:
            val["beta2"] = jnp.sqrt(norms["beta2"] + EPS)
            val["ib2"] = 1.0 / val["beta2"]
            val["k3"] = val["beta2"] * val["k1"]

    def tiles2():
        after1()
        return square_sum([fb[1, s, yrows(0), :] * val["ib2"] - fb[0, s, yrows(0), :] * val["k3"] for s in range(2)])

    def after2():
        if "ia2" not in val:
            val["alpha2"] = jnp.sqrt(norms["alpha2"] + EPS)
            val["ia2"] = 1.0 / val["alpha2"]

    def tiles3():
        after2()
        ratio = val["alpha2"] * val["ib2"]
        return square_sum([own_rows(ff.at[1, s]) * val["ia2"] - own_update(s) * ratio for s in range(2)])

    def work(s):
        yield from adjoint(0, s)
        yield [], [("fb", 0, s, h) for h in range(Y_SUBS)]
        set_operand(s, lambda b: fb[0, s, :, lanes(b)])
        yield from forward(0, s)
        yield [], [("x", 0)] + [("ff", 0, s, h) for h in range(SUBS)]
        after0()
        set_weights(s, ff[0, s] * val["k1"] - u[s] * val["k2"])
        yield from adjoint(1, s)
        yield [], [("x", 1)] + [("fb", 1, s, h) for h in range(Y_SUBS)]
        after1()
        set_operand(s, lambda b: fb[1, s, :, lanes(b)] * val["ib2"] - fb[0, s, :, lanes(b)] * val["k3"])
        yield from forward(1, s)

    def finish():
        yield [], [("x", 3)]
        beta1, alpha1, beta2, alpha2 = val["beta1"], val["alpha1"], val["beta2"], val["alpha2"]
        beta3 = jnp.sqrt(norms["beta3"] + EPS)
        rho1 = jnp.sqrt(alpha1 * alpha1 + beta2 * beta2)
        cos1, sin1 = alpha1 / rho1, beta2 / rho1
        gain1 = cos1 * beta1 / rho1
        ratio = sin1 * alpha2 / rho1
        rho_bar = -cos1 * alpha2
        rho2 = jnp.sqrt(rho_bar * rho_bar + beta3 * beta3)
        gain2 = rho_bar / rho2 * (sin1 * beta1) / rho2
        first, second = (gain1 - gain2 * ratio) * val["k1"], gain2 * val["ia2"]
        second_a, second_b = second * val["ib2"], first - second * val["k3"]
        for part in range(2):
            for b in range(12):
                rows = pl.ds(64 * part, 64)
                block = jnp.concatenate(
                    [fb[1, s, rows, lanes(b)] * second_a + fb[0, s, rows, lanes(b)] * second_b for s in range(2)], axis=0)
                length = 128 if b < 11 else LAST
                sol[pl.ds(256 * b + part, length, 2), :] = block.T[:length]
        plan.now += 1.0
        yield [], [("ff", 1, s, h) for s in range(2) for h in range(SUBS)]
        lane = lax.broadcasted_iota(jnp.int32, (N, 128), 1)
        out = [
            u[s, pl.ds(0, N), :] - ff[0, s, pl.ds(0, N), :] * first - ff[1, s, pl.ds(0, N), :] * second
            for s in range(2)
        ]
        res[pl.ds(0, N, 2), :] = jnp.where(lane < 64, out[0], pltpu.roll(out[1], 64, 1))
        res[pl.ds(1, N, 2), :] = jnp.where(lane < 64, pltpu.roll(out[0], 64, 1), out[1])
        plan.now += 0.5

    both = [(s, h) for s in range(2) for h in range(SUBS)]
    both_y = [(s, h) for s in range(2) for h in range(Y_SUBS)]
    streams = [z_phase(it, s, h) for it in range(2) for s, h in both]
    streams += [y_phase(it, s, h) for it in range(2) for s, h in both_y]
    streams.append(exchange(0, ("beta1", "alpha1"), [("own_y", 0, s, h) for s, h in both_y], tiles0))
    streams.append(exchange(1, ("beta2",), [("x", 0)] + [("own_z", 0, s, h) for s, h in both], tiles1))
    streams.append(exchange(2, ("alpha2",), [("x", 1)] + [("own_y", 1, s, h) for s, h in both_y], tiles2))
    streams.append(exchange(3, ("beta3",), [("x", 2)] + [("own_z", 1, s, h) for s, h in both], tiles3))
    streams += [work(0), work(1), finish()]
    plan.run(streams)
    assert len(sent) <= MESSAGES
    for copy in sent:
        copy.wait_send()


def shards(operator, recorded):
    op = jnp.transpose(operator[0], (1, 0, 2))
    rec = jnp.transpose(recorded[0], (1, 0, 2)).reshape(2 * N, 128)
    vmem = pl.BlockSpec(memory_space=pltpu.VMEM)
    out = jax.ShapeDtypeStruct((2 * N, 128), F32)
    sol, res = pl.pallas_call(
        kernel,
        out_shape=[out, out],
        in_specs=[pl.BlockSpec(memory_space=pl.ANY), vmem],
        out_specs=[vmem, vmem],
        scratch_shapes=[
            pltpu.VMEM((12, 2 * NP, 128), BF16),
            pltpu.VMEM((2 * N, LAST), BF16),
            pltpu.VMEM((2 * NP, 128), F32),
            pltpu.VMEM((2, 2 * ZC, 128), F32),
            pltpu.VMEM((2, NP, 128), F32),
            pltpu.VMEM((2, 128, 2 * NP), BF16),
            pltpu.VMEM((2, NP, 128), BF16),
            pltpu.VMEM((2, 2, 128, NP), F32),
            pltpu.VMEM((2, 2, 128, NP), F32),
            pltpu.VMEM((2, 2, NP, 128), F32),
            pltpu.VMEM((2, 2, NP, 128), F32),
            pltpu.VMEM((2, 2, SUBS, 2, ZC // SUBS // 2, 128), F32),
            pltpu.VMEM((2, 2, SUBS, 2, 3, ZC // SUBS, 128), F32),
            pltpu.VMEM((2, 2, Y_SUBS, 64, NP // Y_SUBS), F32),
            pltpu.VMEM((2, 2, Y_SUBS, 2, 8, NP // Y_SUBS), F32),
            pltpu.VMEM((2, 2, Y_SUBS, 3, 16, NP // Y_SUBS), F32),
            pltpu.VMEM((4, 3, 16, 128), F32),
            pltpu.VMEM((4, 8, 16, 128), F32),
            pltpu.VMEM((4, 8, 16, 128), F32),
            pltpu.VMEM((4, 4, 16, 128), F32),
            pltpu.SemaphoreType.DMA((12,)),
            pltpu.SemaphoreType.DMA((MESSAGES,)),
            pltpu.SemaphoreType.DMA((MESSAGES,)),
        ],
        compiler_params=pltpu.CompilerParams(
            collective_id=0, has_side_effects=True, vmem_limit_bytes=48 * 2**20),
        cost_estimate=pl.CostEstimate(flops=9_437_184_000, bytes_accessed=13_000_000, transcendentals=0),
    )(op, rec)
    return tuple(jnp.transpose(o.reshape(N, 2, 128), (1, 0, 2))[None] for o in (sol, res))


def solution(mesh):
    in_specs = (P("freq", None, "row", "col"), P("freq", None, "row", None))
    out_specs = (P("freq", None, "col", None), P("freq", None, "row", None))
    return jax.shard_map(shards, mesh=mesh, in_specs=in_specs, out_specs=out_specs, check_vma=False)
```

time: 722 us -> 134 us (0.19)
  blocking collectives: 324 us -> 0 us
  waiting for transfers between devices: 294 us -> 0 us
  Pallas kernels: 0 us -> 129 us
  local copies, waits for them, and re-layouts: 36.7 us -> 3.38 us
  matrix products: 27.7 us -> 0 us
  other arithmetic: 20.9 us -> 0 us
  between operations: 17.7 us -> 0.65 us
    psum x5 -> x0, blocking collectives: 324 us -> none  [the longest x2 135 us: forward_reduce(): squares = lax.psum(jnp.sum(update * update), ('freq', 'row'))]
    psum x4 -> x0, waiting for transfers between devices: 294 us -> none  [the longest x2 165 us: forward_reduce(): imaged = lax.psum(partial_value, 'col')]
    pallas_call x0 -> x1, Pallas kernels: none -> 129 us  [shards(): pl.pallas_call(kernel, out_shape=[out, out], in_specs=[pl.BlockSpec(memor...]
    dot_general x4 -> x0, matrix products: 27.7 us -> none  [the longest x2 14.5 us: adjoint_part(): jnp.einsum('krc,lrs->klcs', operator[0], vector[0], preferred_element_typ...]
    squeeze x1 -> x0, local copies, waits for them, and re-layouts: 23.8 us -> none  [adjoint_part(): operator[0]]
    reduce_sum x5 -> x0, other arithmetic: 12.4 us -> none  [the longest x2 5.36 us: forward_reduce(): squares = lax.psum(jnp.sum(update * update), ('freq', 'row'))]
    unnamed x8 -> x4, local copies, waits for them, and re-layouts: 12.9 us -> 3.38 us
  transfers between devices with their start and end apart: 4 -> 0, of which waited for: 4 -> 0; matrix products, arithmetic and copies ran while one was open for 0% -> 0% of each run, Pallas kernels for 0% -> 0%
where the time goes in v2:
time: 134 us; the launch traced here: 133 us
  Pallas kernels  129 us (96%)
  local copies, waits for them, and re-layouts  3.38 us (3%)
    pallas_call x1, Pallas kernels, shards(): pl.pallas_call(kernel, out_shape=[out, out], in_specs=[pl.BlockSpec(memor...  129 us
    unnamed x4, local copies, waits for them, and re-layouts  3.38 us

profile of v2, /device:TPU:1, one launch (start us, length us, event | category | flops | bytes accessed | tf_op | source)
XLA Modules:
  0.0 133.0 jit_solution(17631157620702411377)
XLA Ops:
  0.6 0.0 copy-start
  0.6 1.1 copy-done
  1.8 128.9 %shard_map.41 = (f32[3000,128]{1,0:T(8,128)S(1)}, f32[3000,128]{1,0:T(8,128)S(1)}) custom-call(bf16[1500,2,1500]{2,1,0:T(2,128)(2,1)} %bitcast.21, bf16[3000,128]{1,0:T(8,128)(2,1)S(1)} %bitcast.20), custom_call_target="tpu_custom_call" | custom-call | flops 9437184000 | bytes 13000000 | tf_op jit(solution)/shard_map/pallas_call | solution.py:459
  130.7 1.1 copy.6
  131.8 1.1 copy.7
Async XLA Ops:
  0.6 1.1 copy-start

commit v3 on v2

--- a/solution.py
+++ b/solution.py
@@ -18,8 +18,10 @@
 SUBS = 2
 Y_SUBS = 2
 Y_DIRECT = False
-LAT = 2.3
-RS_SHORT = False
+LAT = 2.8
+X_LAT = 3.6
+BEHIND = 64
+RS_SHORT = True
 AG_SHORT = False
 
 
@@ -75,7 +77,7 @@
                 del waiting[place]
 
 
-def kernel(op_hbm, rec, sol, res, en, tail, xs, xc, u, wt, z, pb, fb, pf, ff, rzh, rzf, ryc, ryh, ryf,
+def kernel(op_hbm, rec_hbm, sol, res, rec, en, tail, xs, xc, u, wt, z, pb, fb, pf, ff, rzh, rzf, ryc, ryh, ryf,
            sbuf, rrow, rcol, rfreq, load_sem, send_sem, recv_sem):
     freq, row, col = lax.axis_index("freq"), lax.axis_index("row"), lax.axis_index("col")
     y, q = row // 2, row % 2
@@ -87,6 +89,8 @@
         for j in range(11)
     ]
     loads.append(pltpu.make_async_copy(source.at[:, pl.ds(1408, LAST)], tail, load_sem.at[11]))
+    recorded = pltpu.make_async_copy(rec_hbm, rec, load_sem.at[12])
+    recorded.start()
     for c in loads:
         c.start()
 
@@ -110,6 +114,8 @@
             device_id=peer, device_id_type=MESH)
         copy.start()
         sent.append(copy)
+        if len(sent) > BEHIND:
+            sent[-1 - BEHIND].wait_send()
         return k
 
     def arrive(k, dst):
@@ -272,7 +278,7 @@
             slots[n, me, pl.ds(0, rows), :] = value
             order = sorted(range(size - 1), key=lambda k: abs(2 * k + 2 - size))
             keys = {
-                k: message(sbuf.at[n, stage, pl.ds(0, rows)], slots.at[n, me, pl.ds(0, rows)], group[k], (), hops)
+                k: message(sbuf.at[n, stage, pl.ds(0, rows)], slots.at[n, me, pl.ds(0, rows)], group[k], (), hops, X_LAT)
                 for k in order
             }
             yield list(keys.values()), []
@@ -336,6 +342,7 @@
             plan.now += 0.4 * count
             mark("pf", it, s, group)
 
+    recorded.wait()
     xs[pl.ds(0, 2 * N), :] = rec[...].astype(F32)
     xs[pl.ds(2 * N, 72), :] = jnp.zeros((72, 128), F32)
     lane = lax.broadcasted_iota(jnp.int32, (NP, 128), 1)
@@ -447,7 +454,7 @@
     streams += [work(0), work(1), finish()]
     plan.run(streams)
     assert len(sent) <= MESSAGES
-    for copy in sent:
+    for copy in sent[-BEHIND:]:
         copy.wait_send()
 
 
@@ -459,9 +466,10 @@
     sol, res = pl.pallas_call(
         kernel,
         out_shape=[out, out],
-        in_specs=[pl.BlockSpec(memory_space=pl.ANY), vmem],
+        in_specs=[pl.BlockSpec(memory_space=pl.ANY)] * 2,
         out_specs=[vmem, vmem],
         scratch_shapes=[
+            pltpu.VMEM((2 * N, 128), BF16),
             pltpu.VMEM((12, 2 * NP, 128), BF16),
             pltpu.VMEM((2 * N, LAST), BF16),
             pltpu.VMEM((2 * NP, 128), F32),
@@ -482,7 +490,7 @@
             pltpu.VMEM((4, 8, 16, 128), F32),
             pltpu.VMEM((4, 8, 16, 128), F32),
             pltpu.VMEM((4, 4, 16, 128), F32),
-            pltpu.SemaphoreType.DMA((12,)),
+            pltpu.SemaphoreType.DMA((13,)),
             pltpu.SemaphoreType.DMA((MESSAGES,)),
             pltpu.SemaphoreType.DMA((MESSAGES,)),
         ],

time: 134 us -> 131 us (0.978)
  Pallas kernels: 129 us -> 127 us
    pallas_call x1, Pallas kernels: 129 us -> 127 us  [shards(): pl.pallas_call(kernel, out_shape=[out, out], in_specs=[pl.BlockSpec(memor...]
where the time goes in v3:
time: 131 us
  Pallas kernels  127 us (97%)
  local copies, waits for them, and re-layouts  3.38 us (3%)
    pallas_call x1, Pallas kernels, shards(): pl.pallas_call(kernel, out_shape=[out, out], in_specs=[pl.BlockSpec(memor...  127 us
    unnamed x4, local copies, waits for them, and re-layouts  3.38 us

profile of v3, /device:TPU:1, one launch (start us, length us, event | category | flops | bytes accessed | tf_op | source)
XLA Modules:
  0.0 131.3 jit_solution(18300634941135228001)
XLA Ops:
  0.6 0.0 copy-start
  0.6 1.1 copy-done
  1.8 127.3 %shard_map.41 = (f32[3000,128]{1,0:T(8,128)S(1)}, f32[3000,128]{1,0:T(8,128)S(1)}) custom-call(bf16[1500,2,1500]{2,1,0:T(2,128)(2,1)} %bitcast.21, bf16[3000,128]{1,0:T(8,128)(2,1)S(1)} %bitcast.20), custom_call_target="tpu_custom_call" | custom-call | flops 9437184000 | bytes 13000000 | tf_op jit(solution)/shard_map/pallas_call | solution.py:466
  129.0 1.1 copy.6
  130.2 1.1 copy.7
Async XLA Ops:
  0.6 1.1 copy-start
